TPU v7x, 128 devices: a whole 4x4x4 slice. The times are simulated.
128 devices in a mesh: ctx: 16 (over x_lo, y, core), ch: 8 (over x_hi, z).
Axes of the slice: x: 4 (x_hi: 2, x_lo: 2; x = x_hi * 2 + x_lo), y: 4, z: 4, core: 2. Of those that a mesh axis runs over, the one named last changes fastest.
Arguments:
- query_branch: bfloat16 [4096, 8192], P('ctx', 'ch'), may hold values from -6 to 6
- key_raw: bfloat16 [4096, 8192], P('ctx', 'ch'), may hold values from -6 to 6
- value_branch: bfloat16 [4096, 8192], P('ctx', 'ch'), may hold values from -6 to 6
- conv_out: bfloat16 [4096, 8192], P('ctx', 'ch'), may hold values from -6 to 6
- out_grad: bfloat16 [4096, 8192], P('ctx', 'ch'), may hold values from -18 to 18
- long_filter: bfloat16 [4096, 8192], P('ctx', 'ch'), may hold values from -0.09375 to 0.09375
- short_filter: float32 [3, 8192], P(None, 'ch'), may hold values from -3 to 3
Outputs:
- query_grad: bfloat16 [4096, 8192], P('ctx', 'ch')
- key_raw_grad: bfloat16 [4096, 8192], P('ctx', 'ch')
- value_grad: bfloat16 [4096, 8192], P('ctx', 'ch')
- filter_grad: float32 [4096, 8192], P('ctx', 'ch')
- short_grad: float32 [3, 8192], P(None, 'ch')
All inputs are finite; a program needn't handle non-finite values.
Results may differ from a plain program's by a relative error of at most 0.0049.
Values may be sent and summed in bfloat16 or wider, within the bound.
A program may use at most 128 MiB of HBM per device.

v0:
```python
import math
import jax
import jax.numpy as jnp
from jax import lax
from jax.sharding import PartitionSpec as P

HIGHEST = lax.Precision.HIGHEST


def shifted(block, axis, distance):
    devices = range(lax.axis_size(axis))
    route = [(i - distance, i) for i in devices if i - distance in devices]
    return lax.ppermute(block, axis, route)


def spectral_tables(block_rows):
    length = 2 * block_rows
    rows_all = jnp.arange(length, dtype=jnp.int32)
    frequency = jnp.where(rows_all <= block_rows, rows_all, rows_all - block_rows)
    cosine_rows = rows_all <= block_rows
    column = jnp.arange(block_rows, dtype=jnp.int32)
    phase_index = frequency[:, None] * column[None, :] % length
    angles = phase_index.astype(jnp.float32) * (math.pi / block_rows)
    forward_table = jnp.where(cosine_rows[:, None], jnp.cos(angles), -jnp.sin(angles))
    upper = lax.optimization_barrier(forward_table.astype(jnp.bfloat16))
    lower = (forward_table - upper.astype(jnp.float32)).astype(jnp.bfloat16)
    forward_pair = jnp.concatenate([upper, lower], axis=1)
    edge = (frequency == 0) | (frequency == block_rows)
    weight = jnp.where(edge, 1.0, 2.0).astype(jnp.float32) / length
    inverse_table = forward_table.T * weight[None, :]
    parity = jnp.where(frequency % 2 == 0, 1.0, -1.0).astype(jnp.float32)[:, None]
    dc_mask = jnp.where(column == 0, 0.0, 1.0).astype(jnp.float32)[:, None]
    return (forward_pair, inverse_table, parity, dc_mask)


def forward(forward_pair, data_block):
    doubled = jnp.concatenate([data_block, data_block], axis=0)
    return jnp.dot(forward_pair, doubled, preferred_element_type=jnp.float32)


def conj_product(left, right, dc_mask):
    half = left.shape[0] // 2
    left_re, left_im = (left[:half], left[half:])
    right_re, right_im = (right[:half], right[half:])
    both_im = left_im * right_im
    real_part = left_re * right_re + dc_mask * both_im
    imag_part = dc_mask * (left_re * right_im - left_im * right_re) + (1.0 - dc_mask) * both_im
    return jnp.concatenate([real_part, imag_part], axis=0)


def sequence_blocks(long_filter, gated, conv_grad, tables):
    forward_pair, inverse_table, parity, dc_mask = tables
    block_rows, local_width = gated.shape
    block_count = lax.axis_size("ctx")
    filters = lax.all_gather(long_filter, "ctx", axis=0, tiled=True)
    gateds = lax.all_gather(gated, "ctx", axis=0, tiled=True)
    spectrum_zero = jnp.zeros((2 * block_rows, local_width), jnp.float32)

    def pair_step(turn_index, carried, grad_block):
        out_acc, lag_acc, prev_filter, prev_gated = carried
        row_start = turn_index * block_rows
        filter_block = lax.dynamic_slice_in_dim(filters, row_start, block_rows, 0)
        gated_block = lax.dynamic_slice_in_dim(gateds, row_start, block_rows, 0)
        spectra = forward(
            forward_pair, jnp.concatenate([filter_block, gated_block, grad_block], axis=1)
        )
        filter_spec = spectra[:, :local_width]
        gated_spec = spectra[:, local_width : 2 * local_width]
        grad_spec = spectra[:, 2 * local_width :]
        out_acc = out_acc + conj_product(filter_spec + parity * prev_filter, grad_spec, dc_mask)
        lag_acc = lag_acc + conj_product(gated_spec + parity * prev_gated, grad_spec, dc_mask)
        return (out_acc, lag_acc, filter_spec, gated_spec)

    initial = (spectrum_zero, spectrum_zero, spectrum_zero, spectrum_zero)

    def cycle_turn(turn_index, status):
        carried, held = status
        carried = pair_step(turn_index, carried, held)
        held = shifted(held, "ctx", -1)
        return (carried, held)

    carried, held = lax.fori_loop(0, block_count - 1, cycle_turn, (initial, conv_grad))
    carried = pair_step(block_count - 1, carried, held)
    out_acc, lag_acc = (carried[0], carried[1])
    paired = jnp.dot(
        inverse_table,
        jnp.concatenate([out_acc, lag_acc], axis=1),
        precision=HIGHEST,
        preferred_element_type=jnp.float32,
    )
    return (paired[:, :local_width], paired[:, local_width:])


def per_device(query_branch, key_raw, value_branch, conv_out, out_grad, long_filter, short_filter):
    block_rows, local_width = query_branch.shape
    tap_count = short_filter.shape[0]
    block_count = lax.axis_size("ctx")
    tables = spectral_tables(block_rows)
    before = shifted(key_raw[block_rows - (tap_count - 1) :], "ctx", 1)
    extended = jnp.concatenate([before, key_raw], axis=0).astype(jnp.float32)
    key_conv = jnp.zeros((block_rows, local_width), jnp.float32)
    for shift_tap in range(tap_count):
        key_conv = (
            key_conv
            + short_filter[shift_tap]
            * extended[tap_count - 1 - shift_tap : tap_count - 1 - shift_tap + block_rows]
        )
    value_wide = value_branch.astype(jnp.float32)
    gated = (key_conv * value_wide).astype(jnp.bfloat16)
    grad_wide = out_grad.astype(jnp.float32)
    query_grad = (grad_wide * conv_out.astype(jnp.float32)).astype(jnp.bfloat16)
    conv_grad = (grad_wide * query_branch.astype(jnp.float32)).astype(jnp.bfloat16)
    gated_grad, lag_grad = sequence_blocks(long_filter, gated, conv_grad, tables)
    value_grad = (gated_grad * key_conv).astype(jnp.bfloat16)
    key_grad = gated_grad * value_wide
    rows_next = shifted(key_grad[: tap_count - 1], "ctx", -1)
    tail_ext = jnp.concatenate([key_grad, rows_next], axis=0)
    raw_total = jnp.zeros((block_rows, local_width), jnp.float32)
    for shift_tap in range(tap_count):
        raw_total = (
            raw_total + short_filter[shift_tap] * tail_ext[shift_tap : shift_tap + block_rows]
        )
    key_raw_grad = raw_total.astype(jnp.bfloat16)
    tap_terms = jnp.stack(
        [
            jnp.sum(
                key_grad
                * extended[tap_count - 1 - shift_tap : tap_count - 1 - shift_tap + block_rows],
                axis=0,
            )
            for shift_tap in range(tap_count)
        ]
    )
    short_grad = lax.psum(tap_terms, "ctx")
    squares = jnp.sum(lag_grad * lag_grad)
    total_squares = lax.psum(squares, ("ctx", "ch"))
    entries = float(block_rows * local_width * block_count * lax.axis_size("ch"))
    scale_factor = lax.rsqrt(total_squares / entries + 1e-06)
    return (query_grad, key_raw_grad, value_grad, lag_grad * scale_factor, short_grad)


def solution(mesh):
    in_specs = (
        P("ctx", "ch"),
        P("ctx", "ch"),
        P("ctx", "ch"),
        P("ctx", "ch"),
        P("ctx", "ch"),
        P("ctx", "ch"),
        P(None, "ch"),
    )
    out_specs = (P("ctx", "ch"), P("ctx", "ch"), P("ctx", "ch"), P("ctx", "ch"), P(None, "ch"))
    return jax.shard_map(
        per_device, mesh=mesh, in_specs=in_specs, out_specs=out_specs, check_vma=False
    )
```

profile of v0, /device:TPU:0, one launch (start us, length us, event | category | flops | bytes accessed | tf_op | source)
XLA Modules:
  0.0 759.4 jit_solution(221422856139085992)
XLA Ops:
  13.7 2.6 fusion.68
  16.3 2.7 subtract_convert_fusion
  21.9 42.5 %all-gather.3.cloned.1.call-done = bf16[4096,1024]{1,0:T(8,128)(2,1)} async-done(((bf16[256,1024]{1,0:T(8,128)(2,1)}), bf16[4096,1024]{1,0:T(8,128)(2,1)}) %all-gather.3.cloned.1.call-update) | async-done | bytes 8388624 | tf_op jit(solution)/shard_map/all_gather | solution.py:55
  66.2 53.5 %all-gather.5.cloned.1.call-done = bf16[4096,1024]{1,0:T(8,128)(2,1)} async-done(((bf16[256,1024]{1,0:T(8,128)(2,1)}), bf16[4096,1024]{1,0:T(8,128)(2,1)}) %all-gather.5.cloned.1.call-update) | async-done | bytes 8388624 | tf_op jit(solution)/shard_map/all_gather | solution.py:56
  124.7 459.0 %while.23 = (s32[]{:T(128)}, f32[512,1024]{1,0:T(8,128)}, f32[512,1024]{1,0:T(8,128)}, f32[512,1024]{1,0:T(8,128)}, f32[512,1024]{1,0:T(8,128)}, /*index=5*/bf16...) while((s32[]{:T(128)}, f32[512,1024]{1,0:T(8,128)}, ...), condition=%wide.region_1.2_spmd.clone.clone, body=%wide.region_0.1_spmd.clone.clone.sunk | while | flops 1639981824 | bytes 53486816 | solution.py:82
  130.1 12.8 %convolution_bitcast_fusion.2 = f32[512,3072]{1,0:T(8,128)S(1)} fusion(bf16[512,512]{1,0:T(8,128)(2,1)} %get-tuple-element.451, bf16[256,1024]{1,0:T(8,128)(2,1)} %copy.23, bf16[256,1024]{1,0:T(8,128)(2,1)S(1)} %constant_dynamic-slice_fusion.4, bf16[256,1024]{1,0:T(8,128)(2,1)S(1)} %constant_dynamic-slice_fusion.5), kind=kOutput, calls=%fused_computation.2.clone.1 | convolution fusion | flops 1629487104 | bytes 8388608 | tf_op jit(solution)/shard_map/while/body/eval_jaxpr/dot_general | solution.py:38
  142.9 5.0 multiply_add_fusion.14
  147.9 1.9 multiply_add_fusion.15
  149.9 4.2 maximum_add_fusion.5
  159.5 12.8 %convolution_bitcast_fusion.2 = f32[512,3072]{1,0:T(8,128)S(1)} fusion(bf16[512,512]{1,0:T(8,128)(2,1)} %get-tuple-element.451, bf16[256,1024]{1,0:T(8,128)(2,1)} %copy.23, bf16[256,1024]{1,0:T(8,128)(2,1)S(1)} %constant_dynamic-slice_fusion.4, bf16[256,1024]{1,0:T(8,128)(2,1)S(1)} %constant_dynamic-slice_fusion.5), kind=kOutput, calls=%fused_computation.2.clone.1 | convolution fusion | flops 1629487104 | bytes 8388608 | tf_op jit(solution)/shard_map/while/body/eval_jaxpr/dot_general | solution.py:38
  172.3 5.0 multiply_add_fusion.14
  177.3 1.9 multiply_add_fusion.15
  179.2 5.6 maximum_add_fusion.5
  190.2 12.8 %convolution_bitcast_fusion.2 = f32[512,3072]{1,0:T(8,128)S(1)} fusion(bf16[512,512]{1,0:T(8,128)(2,1)} %get-tuple-element.451, bf16[256,1024]{1,0:T(8,128)(2,1)} %copy.23, bf16[256,1024]{1,0:T(8,128)(2,1)S(1)} %constant_dynamic-slice_fusion.4, bf16[256,1024]{1,0:T(8,128)(2,1)S(1)} %constant_dynamic-slice_fusion.5), kind=kOutput, calls=%fused_computation.2.clone.1 | convolution fusion | flops 1629487104 | bytes 8388608 | tf_op jit(solution)/shard_map/while/body/eval_jaxpr/dot_general | solution.py:38
  203.0 5.0 multiply_add_fusion.14
  208.0 1.9 multiply_add_fusion.15
  209.9 5.6 maximum_add_fusion.5
  220.9 12.8 %convolution_bitcast_fusion.2 = f32[512,3072]{1,0:T(8,128)S(1)} fusion(bf16[512,512]{1,0:T(8,128)(2,1)} %get-tuple-element.451, bf16[256,1024]{1,0:T(8,128)(2,1)} %copy.23, bf16[256,1024]{1,0:T(8,128)(2,1)S(1)} %constant_dynamic-slice_fusion.4, bf16[256,1024]{1,0:T(8,128)(2,1)S(1)} %constant_dynamic-slice_fusion.5), kind=kOutput, calls=%fused_computation.2.clone.1 | convolution fusion | flops 1629487104 | bytes 8388608 | tf_op jit(solution)/shard_map/while/body/eval_jaxpr/dot_general | solution.py:38
  233.7 5.0 multiply_add_fusion.14
  240.6 5.6 maximum_add_fusion.5
  251.6 12.8 %convolution_bitcast_fusion.2 = f32[512,3072]{1,0:T(8,128)S(1)} fusion(bf16[512,512]{1,0:T(8,128)(2,1)} %get-tuple-element.451, bf16[256,1024]{1,0:T(8,128)(2,1)} %copy.23, bf16[256,1024]{1,0:T(8,128)(2,1)S(1)} %constant_dynamic-slice_fusion.4, bf16[256,1024]{1,0:T(8,128)(2,1)S(1)} %constant_dynamic-slice_fusion.5), kind=kOutput, calls=%fused_computation.2.clone.1 | convolution fusion | flops 1629487104 | bytes 8388608 | tf_op jit(solution)/shard_map/while/body/eval_jaxpr/dot_general | solution.py:38
  264.3 5.0 multiply_add_fusion.14
  269.4 1.9 multiply_add_fusion.15
  271.3 5.6 maximum_add_fusion.5
  282.2 12.8 %convolution_bitcast_fusion.2 = f32[512,3072]{1,0:T(8,128)S(1)} fusion(bf16[512,512]{1,0:T(8,128)(2,1)} %get-tuple-element.451, bf16[256,1024]{1,0:T(8,128)(2,1)} %copy.23, bf16[256,1024]{1,0:T(8,128)(2,1)S(1)} %constant_dynamic-slice_fusion.4, bf16[256,1024]{1,0:T(8,128)(2,1)S(1)} %constant_dynamic-slice_fusion.5), kind=kOutput, calls=%fused_computation.2.clone.1 | convolution fusion | flops 1629487104 | bytes 8388608 | tf_op jit(solution)/shard_map/while/body/eval_jaxpr/dot_general | solution.py:38
  295.0 5.0 multiply_add_fusion.14
  300.1 1.9 multiply_add_fusion.15
  302.0 5.6 maximum_add_fusion.5
  312.9 12.8 %convolution_bitcast_fusion.2 = f32[512,3072]{1,0:T(8,128)S(1)} fusion(bf16[512,512]{1,0:T(8,128)(2,1)} %get-tuple-element.451, bf16[256,1024]{1,0:T(8,128)(2,1)} %copy.23, bf16[256,1024]{1,0:T(8,128)(2,1)S(1)} %constant_dynamic-slice_fusion.4, bf16[256,1024]{1,0:T(8,128)(2,1)S(1)} %constant_dynamic-slice_fusion.5), kind=kOutput, calls=%fused_computation.2.clone.1 | convolution fusion | flops 1629487104 | bytes 8388608 | tf_op jit(solution)/shard_map/while/body/eval_jaxpr/dot_general | solution.py:38
  325.7 5.0 multiply_add_fusion.14
  332.7 5.6 maximum_add_fusion.5
  343.6 12.8 %convolution_bitcast_fusion.2 = f32[512,3072]{1,0:T(8,128)S(1)} fusion(bf16[512,512]{1,0:T(8,128)(2,1)} %get-tuple-element.451, bf16[256,1024]{1,0:T(8,128)(2,1)} %copy.23, bf16[256,1024]{1,0:T(8,128)(2,1)S(1)} %constant_dynamic-slice_fusion.4, bf16[256,1024]{1,0:T(8,128)(2,1)S(1)} %constant_dynamic-slice_fusion.5), kind=kOutput, calls=%fused_computation.2.clone.1 | convolution fusion | flops 1629487104 | bytes 8388608 | tf_op jit(solution)/shard_map/while/body/eval_jaxpr/dot_general | solution.py:38
  356.4 5.0 multiply_add_fusion.14
  363.4 5.6 maximum_add_fusion.5
  374.3 12.8 %convolution_bitcast_fusion.2 = f32[512,3072]{1,0:T(8,128)S(1)} fusion(bf16[512,512]{1,0:T(8,128)(2,1)} %get-tuple-element.451, bf16[256,1024]{1,0:T(8,128)(2,1)} %copy.23, bf16[256,1024]{1,0:T(8,128)(2,1)S(1)} %constant_dynamic-slice_fusion.4, bf16[256,1024]{1,0:T(8,128)(2,1)S(1)} %constant_dynamic-slice_fusion.5), kind=kOutput, calls=%fused_computation.2.clone.1 | convolution fusion | flops 1629487104 | bytes 8388608 | tf_op jit(solution)/shard_map/while/body/eval_jaxpr/dot_general | solution.py:38
  387.1 5.0 multiply_add_fusion.14
  394.1 5.6 maximum_add_fusion.5
  405.0 12.8 %convolution_bitcast_fusion.2 = f32[512,3072]{1,0:T(8,128)S(1)} fusion(bf16[512,512]{1,0:T(8,128)(2,1)} %get-tuple-element.451, bf16[256,1024]{1,0:T(8,128)(2,1)} %copy.23, bf16[256,1024]{1,0:T(8,128)(2,1)S(1)} %constant_dynamic-slice_fusion.4, bf16[256,1024]{1,0:T(8,128)(2,1)S(1)} %constant_dynamic-slice_fusion.5), kind=kOutput, calls=%fused_computation.2.clone.1 | convolution fusion | flops 1629487104 | bytes 8388608 | tf_op jit(solution)/shard_map/while/body/eval_jaxpr/dot_general | solution.py:38
  417.8 5.0 multiply_add_fusion.14
  422.8 1.9 multiply_add_fusion.15
  424.8 5.6 maximum_add_fusion.5
  435.7 12.8 %convolution_bitcast_fusion.2 = f32[512,3072]{1,0:T(8,128)S(1)} fusion(bf16[512,512]{1,0:T(8,128)(2,1)} %get-tuple-element.451, bf16[256,1024]{1,0:T(8,128)(2,1)} %copy.23, bf16[256,1024]{1,0:T(8,128)(2,1)S(1)} %constant_dynamic-slice_fusion.4, bf16[256,1024]{1,0:T(8,128)(2,1)S(1)} %constant_dynamic-slice_fusion.5), kind=kOutput, calls=%fused_computation.2.clone.1 | convolution fusion | flops 1629487104 | bytes 8388608 | tf_op jit(solution)/shard_map/while/body/eval_jaxpr/dot_general | solution.py:38
  448.5 5.0 multiply_add_fusion.14
  453.5 1.9 multiply_add_fusion.15
  455.5 5.6 maximum_add_fusion.5
  466.4 12.8 %convolution_bitcast_fusion.2 = f32[512,3072]{1,0:T(8,128)S(1)} fusion(bf16[512,512]{1,0:T(8,128)(2,1)} %get-tuple-element.451, bf16[256,1024]{1,0:T(8,128)(2,1)} %copy.23, bf16[256,1024]{1,0:T(8,128)(2,1)S(1)} %constant_dynamic-slice_fusion.4, bf16[256,1024]{1,0:T(8,128)(2,1)S(1)} %constant_dynamic-slice_fusion.5), kind=kOutput, calls=%fused_computation.2.clone.1 | convolution fusion | flops 1629487104 | bytes 8388608 | tf_op jit(solution)/shard_map/while/body/eval_jaxpr/dot_general | solution.py:38
  479.2 5.0 multiply_add_fusion.14
  486.1 5.6 maximum_add_fusion.5
  497.1 12.8 %convolution_bitcast_fusion.2 = f32[512,3072]{1,0:T(8,128)S(1)} fusion(bf16[512,512]{1,0:T(8,128)(2,1)} %get-tuple-element.451, bf16[256,1024]{1,0:T(8,128)(2,1)} %copy.23, bf16[256,1024]{1,0:T(8,128)(2,1)S(1)} %constant_dynamic-slice_fusion.4, bf16[256,1024]{1,0:T(8,128)(2,1)S(1)} %constant_dynamic-slice_fusion.5), kind=kOutput, calls=%fused_computation.2.clone.1 | convolution fusion | flops 1629487104 | bytes 8388608 | tf_op jit(solution)/shard_map/while/body/eval_jaxpr/dot_general | solution.py:38
  509.9 5.0 multiply_add_fusion.14
  516.8 5.6 maximum_add_fusion.5
  527.8 12.8 %convolution_bitcast_fusion.2 = f32[512,3072]{1,0:T(8,128)S(1)} fusion(bf16[512,512]{1,0:T(8,128)(2,1)} %get-tuple-element.451, bf16[256,1024]{1,0:T(8,128)(2,1)} %copy.23, bf16[256,1024]{1,0:T(8,128)(2,1)S(1)} %constant_dynamic-slice_fusion.4, bf16[256,1024]{1,0:T(8,128)(2,1)S(1)} %constant_dynamic-slice_fusion.5), kind=kOutput, calls=%fused_computation.2.clone.1 | convolution fusion | flops 1629487104 | bytes 8388608 | tf_op jit(solution)/shard_map/while/body/eval_jaxpr/dot_general | solution.py:38
  540.6 5.0 multiply_add_fusion.14
  547.5 5.6 maximum_add_fusion.5
  558.5 12.8 %convolution_bitcast_fusion.2 = f32[512,3072]{1,0:T(8,128)S(1)} fusion(bf16[512,512]{1,0:T(8,128)(2,1)} %get-tuple-element.451, bf16[256,1024]{1,0:T(8,128)(2,1)} %copy.23, bf16[256,1024]{1,0:T(8,128)(2,1)S(1)} %constant_dynamic-slice_fusion.4, bf16[256,1024]{1,0:T(8,128)(2,1)S(1)} %constant_dynamic-slice_fusion.5), kind=kOutput, calls=%fused_computation.2.clone.1 | convolution fusion | flops 1629487104 | bytes 8388608 | tf_op jit(solution)/shard_map/while/body/eval_jaxpr/dot_general | solution.py:38
  571.3 5.0 multiply_add_fusion.14
  578.2 5.6 maximum_add_fusion.5
  583.8 6.4 fusion.21
  590.2 2.7 slice_add_fusion.1
  596.5 5.8 fusion.17
  603.1 85.2 %psum.14 = f32[]{:T(128)} all-reduce(f32[]{:T(128)} %multiply_reduce_fusion.3), channel_id=1, replica_groups=mesh['ctx'=16,'ch'=8] {'ctx','ch'}, use_global_device_ids=true, to_apply=%region_3.4 | all-reduce | flops 1 | bytes 8 | tf_op jit(solution)/shard_map/psum | solution.py:136
  689.0 3.1 slice_multiply_fusion.2
  694.4 55.0 %psum.15 = f32[3,1024]{1,0:T(4,128)} all-reduce(f32[3,1024]{1,0:T(4,128)S(1)} %pad_maximum_fusion.2), channel_id=1, replica_groups=mesh['ctx'=16,'ch'=8] {'ctx'}, use_global_device_ids=true, to_apply=%region_7.8 | all-reduce | flops 3072 | bytes 24576 | tf_op jit(solution)/shard_map/psum | solution.py:134
  749.3 3.2 fusion.37
  (179 shorter events, 118.2 us)
Async XLA Ops:
  7.2 4.9 copy-start.5
  7.2 57.1 %all-gather.3.cloned.1.call-start = ((), (), s32[]{:S(2)}) async-start(), calls=%async_computation | async-start | bytes 8912896 | tf_op jit(solution)/shard_map/all_gather | solution.py:55
  7.9 111.8 %all-gather.5.cloned.1.call-start = ((), (), s32[]{:S(2)}) async-start(), calls=%async_computation.1 | async-start | bytes 8912896 | tf_op jit(solution)/shard_map/all_gather | solution.py:56
  8.7 2.1 collective-permute-start.1
  12.0 1.6 copy-start.2
  13.6 7.0 copy-start.7
  13.6 7.0 copy-start.8
  13.6 7.0 copy-start.9
  19.0 0.7 copy-start.6
  126.6 27.5 %collective-permute-start = (bf16[256,1024]{1,0:T(8,128)(2,1)}, bf16[256,1024]{1,0:T(8,128)(2,1)}, u32[]{:S(2)}, u32[]{:S(2)}) collective-permute-start(bf16[256,1024]{1,0:T(8,128)(2,1)} %copy.23), channel_id=1, source_target_pairs={{8,0},{16,8},{24,16},{32,24},{40,32},{48,40},{56,48},{64,56},{72,6... | collective-permute-start | bytes 1572872 | tf_op jit(solution)/shard_map/while/body/eval_jaxpr/ppermute | solution.py:13
  156.0 28.8 %collective-permute-start = (bf16[256,1024]{1,0:T(8,128)(2,1)}, bf16[256,1024]{1,0:T(8,128)(2,1)}, u32[]{:S(2)}, u32[]{:S(2)}) collective-permute-start(bf16[256,1024]{1,0:T(8,128)(2,1)} %copy.23), channel_id=1, source_target_pairs={{8,0},{16,8},{24,16},{32,24},{40,32},{48,40},{56,48},{64,56},{72,6... | collective-permute-start | bytes 1572872 | tf_op jit(solution)/shard_map/while/body/eval_jaxpr/ppermute | solution.py:13
  186.7 28.8 %collective-permute-start = (bf16[256,1024]{1,0:T(8,128)(2,1)}, bf16[256,1024]{1,0:T(8,128)(2,1)}, u32[]{:S(2)}, u32[]{:S(2)}) collective-permute-start(bf16[256,1024]{1,0:T(8,128)(2,1)} %copy.23), channel_id=1, source_target_pairs={{8,0},{16,8},{24,16},{32,24},{40,32},{48,40},{56,48},{64,56},{72,6... | collective-permute-start | bytes 1572872 | tf_op jit(solution)/shard_map/while/body/eval_jaxpr/ppermute | solution.py:13
  217.4 28.8 %collective-permute-start = (bf16[256,1024]{1,0:T(8,128)(2,1)}, bf16[256,1024]{1,0:T(8,128)(2,1)}, u32[]{:S(2)}, u32[]{:S(2)}) collective-permute-start(bf16[256,1024]{1,0:T(8,128)(2,1)} %copy.23), channel_id=1, source_target_pairs={{8,0},{16,8},{24,16},{32,24},{40,32},{48,40},{56,48},{64,56},{72,6... | collective-permute-start | bytes 1572872 | tf_op jit(solution)/shard_map/while/body/eval_jaxpr/ppermute | solution.py:13
  248.0 28.8 %collective-permute-start = (bf16[256,1024]{1,0:T(8,128)(2,1)}, bf16[256,1024]{1,0:T(8,128)(2,1)}, u32[]{:S(2)}, u32[]{:S(2)}) collective-permute-start(bf16[256,1024]{1,0:T(8,128)(2,1)} %copy.23), channel_id=1, source_target_pairs={{8,0},{16,8},{24,16},{32,24},{40,32},{48,40},{56,48},{64,56},{72,6... | collective-permute-start | bytes 1572872 | tf_op jit(solution)/shard_map/while/body/eval_jaxpr/ppermute | solution.py:13
  278.7 28.8 %collective-permute-start = (bf16[256,1024]{1,0:T(8,128)(2,1)}, bf16[256,1024]{1,0:T(8,128)(2,1)}, u32[]{:S(2)}, u32[]{:S(2)}) collective-permute-start(bf16[256,1024]{1,0:T(8,128)(2,1)} %copy.23), channel_id=1, source_target_pairs={{8,0},{16,8},{24,16},{32,24},{40,32},{48,40},{56,48},{64,56},{72,6... | collective-permute-start | bytes 1572872 | tf_op jit(solution)/shard_map/while/body/eval_jaxpr/ppermute | solution.py:13
  309.4 28.8 %collective-permute-start = (bf16[256,1024]{1,0:T(8,128)(2,1)}, bf16[256,1024]{1,0:T(8,128)(2,1)}, u32[]{:S(2)}, u32[]{:S(2)}) collective-permute-start(bf16[256,1024]{1,0:T(8,128)(2,1)} %copy.23), channel_id=1, source_target_pairs={{8,0},{16,8},{24,16},{32,24},{40,32},{48,40},{56,48},{64,56},{72,6... | collective-permute-start | bytes 1572872 | tf_op jit(solution)/shard_map/while/body/eval_jaxpr/ppermute | solution.py:13
  340.1 28.8 %collective-permute-start = (bf16[256,1024]{1,0:T(8,128)(2,1)}, bf16[256,1024]{1,0:T(8,128)(2,1)}, u32[]{:S(2)}, u32[]{:S(2)}) collective-permute-start(bf16[256,1024]{1,0:T(8,128)(2,1)} %copy.23), channel_id=1, source_target_pairs={{8,0},{16,8},{24,16},{32,24},{40,32},{48,40},{56,48},{64,56},{72,6... | collective-permute-start | bytes 1572872 | tf_op jit(solution)/shard_map/while/body/eval_jaxpr/ppermute | solution.py:13
  370.8 28.8 %collective-permute-start = (bf16[256,1024]{1,0:T(8,128)(2,1)}, bf16[256,1024]{1,0:T(8,128)(2,1)}, u32[]{:S(2)}, u32[]{:S(2)}) collective-permute-start(bf16[256,1024]{1,0:T(8,128)(2,1)} %copy.23), channel_id=1, source_target_pairs={{8,0},{16,8},{24,16},{32,24},{40,32},{48,40},{56,48},{64,56},{72,6... | collective-permute-start | bytes 1572872 | tf_op jit(solution)/shard_map/while/body/eval_jaxpr/ppermute | solution.py:13
  401.5 28.8 %collective-permute-start = (bf16[256,1024]{1,0:T(8,128)(2,1)}, bf16[256,1024]{1,0:T(8,128)(2,1)}, u32[]{:S(2)}, u32[]{:S(2)}) collective-permute-start(bf16[256,1024]{1,0:T(8,128)(2,1)} %copy.23), channel_id=1, source_target_pairs={{8,0},{16,8},{24,16},{32,24},{40,32},{48,40},{56,48},{64,56},{72,6... | collective-permute-start | bytes 1572872 | tf_op jit(solution)/shard_map/while/body/eval_jaxpr/ppermute | solution.py:13
  432.2 28.8 %collective-permute-start = (bf16[256,1024]{1,0:T(8,128)(2,1)}, bf16[256,1024]{1,0:T(8,128)(2,1)}, u32[]{:S(2)}, u32[]{:S(2)}) collective-permute-start(bf16[256,1024]{1,0:T(8,128)(2,1)} %copy.23), channel_id=1, source_target_pairs={{8,0},{16,8},{24,16},{32,24},{40,32},{48,40},{56,48},{64,56},{72,6... | collective-permute-start | bytes 1572872 | tf_op jit(solution)/shard_map/while/body/eval_jaxpr/ppermute | solution.py:13
  462.9 28.8 %collective-permute-start = (bf16[256,1024]{1,0:T(8,128)(2,1)}, bf16[256,1024]{1,0:T(8,128)(2,1)}, u32[]{:S(2)}, u32[]{:S(2)}) collective-permute-start(bf16[256,1024]{1,0:T(8,128)(2,1)} %copy.23), channel_id=1, source_target_pairs={{8,0},{16,8},{24,16},{32,24},{40,32},{48,40},{56,48},{64,56},{72,6... | collective-permute-start | bytes 1572872 | tf_op jit(solution)/shard_map/while/body/eval_jaxpr/ppermute | solution.py:13
  493.6 28.8 %collective-permute-start = (bf16[256,1024]{1,0:T(8,128)(2,1)}, bf16[256,1024]{1,0:T(8,128)(2,1)}, u32[]{:S(2)}, u32[]{:S(2)}) collective-permute-start(bf16[256,1024]{1,0:T(8,128)(2,1)} %copy.23), channel_id=1, source_target_pairs={{8,0},{16,8},{24,16},{32,24},{40,32},{48,40},{56,48},{64,56},{72,6... | collective-permute-start | bytes 1572872 | tf_op jit(solution)/shard_map/while/body/eval_jaxpr/ppermute | solution.py:13
  524.3 28.8 %collective-permute-start = (bf16[256,1024]{1,0:T(8,128)(2,1)}, bf16[256,1024]{1,0:T(8,128)(2,1)}, u32[]{:S(2)}, u32[]{:S(2)}) collective-permute-start(bf16[256,1024]{1,0:T(8,128)(2,1)} %copy.23), channel_id=1, source_target_pairs={{8,0},{16,8},{24,16},{32,24},{40,32},{48,40},{56,48},{64,56},{72,6... | collective-permute-start | bytes 1572872 | tf_op jit(solution)/shard_map/while/body/eval_jaxpr/ppermute | solution.py:13
  555.0 28.8 %collective-permute-start = (bf16[256,1024]{1,0:T(8,128)(2,1)}, bf16[256,1024]{1,0:T(8,128)(2,1)}, u32[]{:S(2)}, u32[]{:S(2)}) collective-permute-start(bf16[256,1024]{1,0:T(8,128)(2,1)} %copy.23), channel_id=1, source_target_pairs={{8,0},{16,8},{24,16},{32,24},{40,32},{48,40},{56,48},{64,56},{72,6... | collective-permute-start | bytes 1572872 | tf_op jit(solution)/shard_map/while/body/eval_jaxpr/ppermute | solution.py:13
  592.9 1.6 copy-start
  592.9 2.2 copy-start.1
  596.4 92.6 %copy-start.3 = (f32[258,1024]{1,0:T(8,128)S(1)}, f32[258,1024]{1,0:T(8,128)}, u32[]{:S(2)}) copy-start(f32[258,1024]{1,0:T(8,128)} %copy-done.2) | copy-start | bytes 3170308
  692.1 1.0 copy-start.4
  693.1 56.3 %collective-permute-start.2 = (f32[2,1024]{1,0:T(2,128)S(1)}, f32[2,1024]{1,0:T(2,128)S(1)}, u32[]{:S(2)}, u32[]{:S(2)}) collective-permute-start(f32[2,1024]{1,0:T(2,128)S(1)} %slice.190), channel_id=1, source_target_pairs={{8,0},{16,8},{24,16},{32,24},{40,32},{48,40},{56,48},{64,56},{72,6... | collective-permute-start | bytes 24584 | tf_op jit(solution)/shard_map/ppermute | solution.py:13
Sparse Core Ops, SparseCore 0:
  9.7 54.5 all-gather.2
  66.6 53.0 all-gather.4
where the time goes:
time: 763 us; the launch traced here: 759 us
  other arithmetic  209 us (27%)
  matrix products  204 us (27%)
  blocking collectives  140 us (18%)
  waiting for transfers between devices  96.7 us (13%)
  local copies, waits for them, and re-layouts  71.7 us (9%)
  starting transfers between devices  21.8 us (3%)
  between operations  15 us (2%)
    dot_general x16, matrix products, forward(): return jnp.dot(forward_pair, doubled, preferred_element_type=jnp.float32)  198 us
    psum x1, blocking collectives, per_device(): total_squares = lax.psum(squares, ('ctx', 'ch'))  85.2 us
    add x16, other arithmetic, pair_step(): out_acc + conj_product(filter_spec + parity * prev_filter, grad_spec, dc_...  83.3 us
    add x15, other arithmetic, pair_step(): gated_spec + parity * prev_gated  75.7 us
    psum x1, blocking collectives, per_device(): short_grad = lax.psum(tap_terms, 'ctx')  55 us
    all_gather x1, waiting for transfers between devices, sequence_blocks(): gateds = lax.all_gather(gated, 'ctx', axis=0, tiled=True)  53.5 us
    all_gather x1, waiting for transfers between devices, sequence_blocks(): filters = lax.all_gather(long_filter, 'ctx', axis=0, tiled=True)  42.5 us
    add x16, other arithmetic, conj_product(): real_part = left_re * right_re + dc_mask * both_im  29.9 us
  transfers between devices with their start and end apart: 19, of which 2 were waited for; matrix products, arithmetic and copies ran while one was open for 56% of the time, Pallas kernels for 0%

commit v1 on v0

--- a/solution.py
+++ b/solution.py
@@ -52,7 +52,9 @@
     forward_pair, inverse_table, parity, dc_mask = tables
     block_rows, local_width = gated.shape
     block_count = lax.axis_size("ctx")
-    filters = lax.all_gather(long_filter, "ctx", axis=0, tiled=True)
+    filters = jnp.concatenate(
+        lax.all_to_all(jnp.stack([long_filter] * lax.axis_size("ctx")), "ctx", 0, 0), axis=0
+    )
     gateds = lax.all_gather(gated, "ctx", axis=0, tiled=True)
     spectrum_zero = jnp.zeros((2 * block_rows, local_width), jnp.float32)
 

time: 763 us -> 820 us (1.075)
  waiting for transfers between devices: 96.7 us -> 139 us
  starting transfers between devices: 21.8 us -> 30.2 us
    all_to_all x0 -> x1, waiting for transfers between devices: none -> 139 us  [sequence_blocks(): lax.all_to_all(jnp.stack([long_filter] * lax.axis_size('ctx')), 'ctx', 0, 0)]
    all_gather x1, waiting for transfers between devices: 53.5 us -> 0.01 us  [sequence_blocks(): gateds = lax.all_gather(gated, 'ctx', axis=0, tiled=True)]
    all_gather x1 -> x0, waiting for transfers between devices: 42.5 us -> none  [sequence_blocks(): filters = lax.all_gather(long_filter, 'ctx', axis=0, tiled=True)]
    all_to_all x0 -> x1, starting transfers between devices: none -> 8.4 us  [sequence_blocks(): lax.all_to_all(jnp.stack([long_filter] * lax.axis_size('ctx')), 'ctx', 0, 0)]
  transfers between devices with their start and end apart: 19 -> 19, of which waited for: 2 -> 1; matrix products, arithmetic and copies ran while one was open for 56% -> 52% of each run, Pallas kernels for 0% -> 0%
where the time goes in v1:
time: 820 us; the launch traced here: 816 us
  other arithmetic  210 us (26%)
  matrix products  204 us (25%)
  blocking collectives  141 us (17%)
  waiting for transfers between devices  139 us (17%)
  local copies, waits for them, and re-layouts  76 us (9%)
  starting transfers between devices  30.2 us (4%)
  between operations  15 us (2%)
    dot_general x16, matrix products, forward(): return jnp.dot(forward_pair, doubled, preferred_element_type=jnp.float32)  198 us
    all_to_all x1, waiting for transfers between devices, sequence_blocks(): lax.all_to_all(jnp.stack([long_filter] * lax.axis_size('ctx')), 'ctx', 0, 0)  139 us
    psum x1, blocking collectives, per_device(): total_squares = lax.psum(squares, ('ctx', 'ch'))  85.7 us
    add x16, other arithmetic, pair_step(): out_acc + conj_product(filter_spec + parity * prev_filter, grad_spec, dc_...  83.6 us
    add x15, other arithmetic, pair_step(): gated_spec + parity * prev_gated  74.9 us
    psum x1, blocking collectives, per_device(): short_grad = lax.psum(tap_terms, 'ctx')  54.9 us
    add x16, other arithmetic, conj_product(): real_part = left_re * right_re + dc_mask * both_im  30 us
    while x15, local copies, waits for them, and re-layouts  27.9 us
  transfers between devices with their start and end apart: 19, of which 1 were waited for; matrix products, arithmetic and copies ran while one was open for 52% of the time, Pallas kernels for 0%

profile of v1, /device:TPU:0, one launch (start us, length us, event | category | flops | bytes accessed | tf_op | source)
XLA Modules:
  0.0 815.9 jit_solution(14653266721388727177)
XLA Ops:
  11.3 3.0 fusion.40
  14.3 4.3 stack.10
  18.6 8.4 %all-to-all-start = ((bf16[16,256,1024]{2,1,0:T(8,128)(2,1)}), bf16[16,256,1024]{2,1,0:T(8,128)(2,1)}, u32[]{:S(2)}, u32[]{:S(2)}) async-start(bf16[16,256,1024]{2,1,0:T(8,128)(2,1)} %stack.10), calls=%async_computation | async-start | bytes 16777216 | tf_op jit(solution)/shard_map/all_to_all | solution.py:56
  27.1 2.6 fusion.68
  29.8 2.7 subtract_convert_fusion
  35.3 139.2 %all-to-all-done = bf16[16,256,1024]{2,1,0:T(8,128)(2,1)} async-done(((bf16[16,256,1024]{2,1,0:T(8,128)(2,1)}), bf16[16,256,1024]{2,1,0:T(8,128)(2,1)}, u32[]{:S(2)}, u32[]{:S(2)}) %all-to-all-start) | async-done | bytes 8388640 | tf_op jit(solution)/shard_map/all_to_all | solution.py:56
  181.5 458.5 %while.23 = (s32[]{:T(128)}, f32[512,1024]{1,0:T(8,128)}, f32[512,1024]{1,0:T(8,128)}, f32[512,1024]{1,0:T(8,128)}, f32[512,1024]{1,0:T(8,128)}, /*index=5*/bf16...) while((s32[]{:T(128)}, f32[512,1024]{1,0:T(8,128)}, ...), condition=%wide.region_1.2_spmd.clone.clone, body=%wide.region_0.1_spmd.clone.clone.sunk | while | flops 1639981824 | bytes 53486816 | solution.py:84
  186.8 12.8 %convolution_bitcast_fusion.2 = f32[512,3072]{1,0:T(8,128)S(1)} fusion(bf16[512,512]{1,0:T(8,128)(2,1)} %get-tuple-element.451, bf16[256,1024]{1,0:T(8,128)(2,1)} %copy.23, bf16[256,1024]{1,0:T(8,128)(2,1)S(1)} %constant_dynamic-slice_fusion.4, bf16[256,1024]{1,0:T(8,128)(2,1)S(1)} %constant_dynamic-slice_fusion.5), kind=kOutput, calls=%fused_computation.2.clone.1 | convolution fusion | flops 1629487104 | bytes 8388608 | tf_op jit(solution)/shard_map/while/body/eval_jaxpr/dot_general | solution.py:38
  199.6 5.0 multiply_add_fusion.14
  204.6 1.9 multiply_add_fusion.15
  206.5 4.3 maximum_add_fusion.5
  216.2 12.8 %convolution_bitcast_fusion.2 = f32[512,3072]{1,0:T(8,128)S(1)} fusion(bf16[512,512]{1,0:T(8,128)(2,1)} %get-tuple-element.451, bf16[256,1024]{1,0:T(8,128)(2,1)} %copy.23, bf16[256,1024]{1,0:T(8,128)(2,1)S(1)} %constant_dynamic-slice_fusion.4, bf16[256,1024]{1,0:T(8,128)(2,1)S(1)} %constant_dynamic-slice_fusion.5), kind=kOutput, calls=%fused_computation.2.clone.1 | convolution fusion | flops 1629487104 | bytes 8388608 | tf_op jit(solution)/shard_map/while/body/eval_jaxpr/dot_general | solution.py:38
  229.0 5.0 multiply_add_fusion.14
  235.9 5.6 maximum_add_fusion.5
  246.8 12.8 %convolution_bitcast_fusion.2 = f32[512,3072]{1,0:T(8,128)S(1)} fusion(bf16[512,512]{1,0:T(8,128)(2,1)} %get-tuple-element.451, bf16[256,1024]{1,0:T(8,128)(2,1)} %copy.23, bf16[256,1024]{1,0:T(8,128)(2,1)S(1)} %constant_dynamic-slice_fusion.4, bf16[256,1024]{1,0:T(8,128)(2,1)S(1)} %constant_dynamic-slice_fusion.5), kind=kOutput, calls=%fused_computation.2.clone.1 | convolution fusion | flops 1629487104 | bytes 8388608 | tf_op jit(solution)/shard_map/while/body/eval_jaxpr/dot_general | solution.py:38
  259.6 5.0 multiply_add_fusion.14
  264.6 1.9 multiply_add_fusion.15
  266.5 5.6 maximum_add_fusion.5
  277.5 12.8 %convolution_bitcast_fusion.2 = f32[512,3072]{1,0:T(8,128)S(1)} fusion(bf16[512,512]{1,0:T(8,128)(2,1)} %get-tuple-element.451, bf16[256,1024]{1,0:T(8,128)(2,1)} %copy.23, bf16[256,1024]{1,0:T(8,128)(2,1)S(1)} %constant_dynamic-slice_fusion.4, bf16[256,1024]{1,0:T(8,128)(2,1)S(1)} %constant_dynamic-slice_fusion.5), kind=kOutput, calls=%fused_computation.2.clone.1 | convolution fusion | flops 1629487104 | bytes 8388608 | tf_op jit(solution)/shard_map/while/body/eval_jaxpr/dot_general | solution.py:38
  290.3 5.0 multiply_add_fusion.14
  295.3 1.9 multiply_add_fusion.15
  297.2 5.6 maximum_add_fusion.5
  308.1 12.8 %convolution_bitcast_fusion.2 = f32[512,3072]{1,0:T(8,128)S(1)} fusion(bf16[512,512]{1,0:T(8,128)(2,1)} %get-tuple-element.451, bf16[256,1024]{1,0:T(8,128)(2,1)} %copy.23, bf16[256,1024]{1,0:T(8,128)(2,1)S(1)} %constant_dynamic-slice_fusion.4, bf16[256,1024]{1,0:T(8,128)(2,1)S(1)} %constant_dynamic-slice_fusion.5), kind=kOutput, calls=%fused_computation.2.clone.1 | convolution fusion | flops 1629487104 | bytes 8388608 | tf_op jit(solution)/shard_map/while/body/eval_jaxpr/dot_general | solution.py:38
  320.9 5.0 multiply_add_fusion.14
  327.8 5.6 maximum_add_fusion.5
  338.8 12.8 %convolution_bitcast_fusion.2 = f32[512,3072]{1,0:T(8,128)S(1)} fusion(bf16[512,512]{1,0:T(8,128)(2,1)} %get-tuple-element.451, bf16[256,1024]{1,0:T(8,128)(2,1)} %copy.23, bf16[256,1024]{1,0:T(8,128)(2,1)S(1)} %constant_dynamic-slice_fusion.4, bf16[256,1024]{1,0:T(8,128)(2,1)S(1)} %constant_dynamic-slice_fusion.5), kind=kOutput, calls=%fused_computation.2.clone.1 | convolution fusion | flops 1629487104 | bytes 8388608 | tf_op jit(solution)/shard_map/while/body/eval_jaxpr/dot_general | solution.py:38
  351.6 5.0 multiply_add_fusion.14
  356.6 1.9 multiply_add_fusion.15
  358.5 5.6 maximum_add_fusion.5
  369.4 12.8 %convolution_bitcast_fusion.2 = f32[512,3072]{1,0:T(8,128)S(1)} fusion(bf16[512,512]{1,0:T(8,128)(2,1)} %get-tuple-element.451, bf16[256,1024]{1,0:T(8,128)(2,1)} %copy.23, bf16[256,1024]{1,0:T(8,128)(2,1)S(1)} %constant_dynamic-slice_fusion.4, bf16[256,1024]{1,0:T(8,128)(2,1)S(1)} %constant_dynamic-slice_fusion.5), kind=kOutput, calls=%fused_computation.2.clone.1 | convolution fusion | flops 1629487104 | bytes 8388608 | tf_op jit(solution)/shard_map/while/body/eval_jaxpr/dot_general | solution.py:38
  382.2 5.0 multiply_add_fusion.14
  387.2 1.9 multiply_add_fusion.15
  389.2 5.6 maximum_add_fusion.5
  400.1 12.8 %convolution_bitcast_fusion.2 = f32[512,3072]{1,0:T(8,128)S(1)} fusion(bf16[512,512]{1,0:T(8,128)(2,1)} %get-tuple-element.451, bf16[256,1024]{1,0:T(8,128)(2,1)} %copy.23, bf16[256,1024]{1,0:T(8,128)(2,1)S(1)} %constant_dynamic-slice_fusion.4, bf16[256,1024]{1,0:T(8,128)(2,1)S(1)} %constant_dynamic-slice_fusion.5), kind=kOutput, calls=%fused_computation.2.clone.1 | convolution fusion | flops 1629487104 | bytes 8388608 | tf_op jit(solution)/shard_map/while/body/eval_jaxpr/dot_general | solution.py:38
  412.9 5.0 multiply_add_fusion.14
  419.8 5.6 maximum_add_fusion.5
  430.8 12.8 %convolution_bitcast_fusion.2 = f32[512,3072]{1,0:T(8,128)S(1)} fusion(bf16[512,512]{1,0:T(8,128)(2,1)} %get-tuple-element.451, bf16[256,1024]{1,0:T(8,128)(2,1)} %copy.23, bf16[256,1024]{1,0:T(8,128)(2,1)S(1)} %constant_dynamic-slice_fusion.4, bf16[256,1024]{1,0:T(8,128)(2,1)S(1)} %constant_dynamic-slice_fusion.5), kind=kOutput, calls=%fused_computation.2.clone.1 | convolution fusion | flops 1629487104 | bytes 8388608 | tf_op jit(solution)/shard_map/while/body/eval_jaxpr/dot_general | solution.py:38
  443.6 5.0 multiply_add_fusion.14
  450.5 5.6 maximum_add_fusion.5
  461.4 12.8 %convolution_bitcast_fusion.2 = f32[512,3072]{1,0:T(8,128)S(1)} fusion(bf16[512,512]{1,0:T(8,128)(2,1)} %get-tuple-element.451, bf16[256,1024]{1,0:T(8,128)(2,1)} %copy.23, bf16[256,1024]{1,0:T(8,128)(2,1)S(1)} %constant_dynamic-slice_fusion.4, bf16[256,1024]{1,0:T(8,128)(2,1)S(1)} %constant_dynamic-slice_fusion.5), kind=kOutput, calls=%fused_computation.2.clone.1 | convolution fusion | flops 1629487104 | bytes 8388608 | tf_op jit(solution)/shard_map/while/body/eval_jaxpr/dot_general | solution.py:38
  474.2 5.0 multiply_add_fusion.14
  481.1 5.6 maximum_add_fusion.5
  492.1 12.8 %convolution_bitcast_fusion.2 = f32[512,3072]{1,0:T(8,128)S(1)} fusion(bf16[512,512]{1,0:T(8,128)(2,1)} %get-tuple-element.451, bf16[256,1024]{1,0:T(8,128)(2,1)} %copy.23, bf16[256,1024]{1,0:T(8,128)(2,1)S(1)} %constant_dynamic-slice_fusion.4, bf16[256,1024]{1,0:T(8,128)(2,1)S(1)} %constant_dynamic-slice_fusion.5), kind=kOutput, calls=%fused_computation.2.clone.1 | convolution fusion | flops 1629487104 | bytes 8388608 | tf_op jit(solution)/shard_map/while/body/eval_jaxpr/dot_general | solution.py:38
  504.9 5.0 multiply_add_fusion.14
  511.8 5.6 maximum_add_fusion.5
  522.7 12.8 %convolution_bitcast_fusion.2 = f32[512,3072]{1,0:T(8,128)S(1)} fusion(bf16[512,512]{1,0:T(8,128)(2,1)} %get-tuple-element.451, bf16[256,1024]{1,0:T(8,128)(2,1)} %copy.23, bf16[256,1024]{1,0:T(8,128)(2,1)S(1)} %constant_dynamic-slice_fusion.4, bf16[256,1024]{1,0:T(8,128)(2,1)S(1)} %constant_dynamic-slice_fusion.5), kind=kOutput, calls=%fused_computation.2.clone.1 | convolution fusion | flops 1629487104 | bytes 8388608 | tf_op jit(solution)/shard_map/while/body/eval_jaxpr/dot_general | solution.py:38
  535.5 5.0 multiply_add_fusion.14
  542.4 5.6 maximum_add_fusion.5
  553.4 12.8 %convolution_bitcast_fusion.2 = f32[512,3072]{1,0:T(8,128)S(1)} fusion(bf16[512,512]{1,0:T(8,128)(2,1)} %get-tuple-element.451, bf16[256,1024]{1,0:T(8,128)(2,1)} %copy.23, bf16[256,1024]{1,0:T(8,128)(2,1)S(1)} %constant_dynamic-slice_fusion.4, bf16[256,1024]{1,0:T(8,128)(2,1)S(1)} %constant_dynamic-slice_fusion.5), kind=kOutput, calls=%fused_computation.2.clone.1 | convolution fusion | flops 1629487104 | bytes 8388608 | tf_op jit(solution)/shard_map/while/body/eval_jaxpr/dot_general | solution.py:38
  566.2 5.0 multiply_add_fusion.14
  573.1 5.6 maximum_add_fusion.5
  584.0 12.8 %convolution_bitcast_fusion.2 = f32[512,3072]{1,0:T(8,128)S(1)} fusion(bf16[512,512]{1,0:T(8,128)(2,1)} %get-tuple-element.451, bf16[256,1024]{1,0:T(8,128)(2,1)} %copy.23, bf16[256,1024]{1,0:T(8,128)(2,1)S(1)} %constant_dynamic-slice_fusion.4, bf16[256,1024]{1,0:T(8,128)(2,1)S(1)} %constant_dynamic-slice_fusion.5), kind=kOutput, calls=%fused_computation.2.clone.1 | convolution fusion | flops 1629487104 | bytes 8388608 | tf_op jit(solution)/shard_map/while/body/eval_jaxpr/dot_general | solution.py:38
  596.8 5.0 multiply_add_fusion.14
  603.8 5.6 maximum_add_fusion.5
  614.7 12.8 %convolution_bitcast_fusion.2 = f32[512,3072]{1,0:T(8,128)S(1)} fusion(bf16[512,512]{1,0:T(8,128)(2,1)} %get-tuple-element.451, bf16[256,1024]{1,0:T(8,128)(2,1)} %copy.23, bf16[256,1024]{1,0:T(8,128)(2,1)S(1)} %constant_dynamic-slice_fusion.4, bf16[256,1024]{1,0:T(8,128)(2,1)S(1)} %constant_dynamic-slice_fusion.5), kind=kOutput, calls=%fused_computation.2.clone.1 | convolution fusion | flops 1629487104 | bytes 8388608 | tf_op jit(solution)/shard_map/while/body/eval_jaxpr/dot_general | solution.py:38
  627.5 5.0 multiply_add_fusion.14
  634.4 5.6 maximum_add_fusion.5
  640.0 6.3 fusion.21
  646.3 2.7 slice_add_fusion.1
  652.6 5.8 fusion.17
  659.2 85.7 %psum.14 = f32[]{:T(128)} all-reduce(f32[]{:T(128)} %multiply_reduce_fusion.3), channel_id=1, replica_groups=mesh['ctx'=16,'ch'=8] {'ctx','ch'}, use_global_device_ids=true, to_apply=%region_3.4 | all-reduce | flops 1 | bytes 8 | tf_op jit(solution)/shard_map/psum | solution.py:138
  745.6 3.1 slice_multiply_fusion.2
  750.9 54.9 %psum.15 = f32[3,1024]{1,0:T(4,128)} all-reduce(f32[3,1024]{1,0:T(4,128)S(1)} %pad_maximum_fusion.2), channel_id=1, replica_groups=mesh['ctx'=16,'ch'=8] {'ctx'}, use_global_device_ids=true, to_apply=%region_7.8 | all-reduce | flops 3072 | bytes 24576 | tf_op jit(solution)/shard_map/psum | solution.py:136
  805.9 3.2 fusion.37
  (179 shorter events, 119.8 us)
Async XLA Ops:
  7.2 169.3 %all-gather.2.cloned.1.call-start = ((), (), s32[]{:S(2)}) async-start(), calls=%async_computation.1 | async-start | bytes 8912896 | tf_op jit(solution)/shard_map/all_gather | solution.py:58
  7.9 2.1 collective-permute-start.1
  11.3 3.0 copy-start.2
  11.3 3.0 copy-start.6
  18.6 155.9 %all-to-all-start = ((bf16[16,256,1024]{2,1,0:T(8,128)(2,1)}), bf16[16,256,1024]{2,1,0:T(8,128)(2,1)}, u32[]{:S(2)}, u32[]{:S(2)}) async-start(bf16[16,256,1024]{2,1,0:T(8,128)(2,1)} %stack.10), calls=%async_computation | async-start | bytes 16777216 | tf_op jit(solution)/shard_map/all_to_all | solution.py:56
  27.0 6.9 copy-start.7
  27.0 6.9 copy-start.8
  27.0 6.9 copy-start.9
  32.4 0.7 copy-start.5
  183.3 27.5 %collective-permute-start = (bf16[256,1024]{1,0:T(8,128)(2,1)}, bf16[256,1024]{1,0:T(8,128)(2,1)}, u32[]{:S(2)}, u32[]{:S(2)}) collective-permute-start(bf16[256,1024]{1,0:T(8,128)(2,1)} %copy.23), channel_id=1, source_target_pairs={{8,0},{16,8},{24,16},{32,24},{40,32},{48,40},{56,48},{64,56},{72,6... | collective-permute-start | bytes 1572872 | tf_op jit(solution)/shard_map/while/body/eval_jaxpr/ppermute | solution.py:13
  212.7 28.8 %collective-permute-start = (bf16[256,1024]{1,0:T(8,128)(2,1)}, bf16[256,1024]{1,0:T(8,128)(2,1)}, u32[]{:S(2)}, u32[]{:S(2)}) collective-permute-start(bf16[256,1024]{1,0:T(8,128)(2,1)} %copy.23), channel_id=1, source_target_pairs={{8,0},{16,8},{24,16},{32,24},{40,32},{48,40},{56,48},{64,56},{72,6... | collective-permute-start | bytes 1572872 | tf_op jit(solution)/shard_map/while/body/eval_jaxpr/ppermute | solution.py:13
  243.3 28.8 %collective-permute-start = (bf16[256,1024]{1,0:T(8,128)(2,1)}, bf16[256,1024]{1,0:T(8,128)(2,1)}, u32[]{:S(2)}, u32[]{:S(2)}) collective-permute-start(bf16[256,1024]{1,0:T(8,128)(2,1)} %copy.23), channel_id=1, source_target_pairs={{8,0},{16,8},{24,16},{32,24},{40,32},{48,40},{56,48},{64,56},{72,6... | collective-permute-start | bytes 1572872 | tf_op jit(solution)/shard_map/while/body/eval_jaxpr/ppermute | solution.py:13
  274.0 28.8 %collective-permute-start = (bf16[256,1024]{1,0:T(8,128)(2,1)}, bf16[256,1024]{1,0:T(8,128)(2,1)}, u32[]{:S(2)}, u32[]{:S(2)}) collective-permute-start(bf16[256,1024]{1,0:T(8,128)(2,1)} %copy.23), channel_id=1, source_target_pairs={{8,0},{16,8},{24,16},{32,24},{40,32},{48,40},{56,48},{64,56},{72,6... | collective-permute-start | bytes 1572872 | tf_op jit(solution)/shard_map/while/body/eval_jaxpr/ppermute | solution.py:13
  304.6 28.8 %collective-permute-start = (bf16[256,1024]{1,0:T(8,128)(2,1)}, bf16[256,1024]{1,0:T(8,128)(2,1)}, u32[]{:S(2)}, u32[]{:S(2)}) collective-permute-start(bf16[256,1024]{1,0:T(8,128)(2,1)} %copy.23), channel_id=1, source_target_pairs={{8,0},{16,8},{24,16},{32,24},{40,32},{48,40},{56,48},{64,56},{72,6... | collective-permute-start | bytes 1572872 | tf_op jit(solution)/shard_map/while/body/eval_jaxpr/ppermute | solution.py:13
  335.3 28.8 %collective-permute-start = (bf16[256,1024]{1,0:T(8,128)(2,1)}, bf16[256,1024]{1,0:T(8,128)(2,1)}, u32[]{:S(2)}, u32[]{:S(2)}) collective-permute-start(bf16[256,1024]{1,0:T(8,128)(2,1)} %copy.23), channel_id=1, source_target_pairs={{8,0},{16,8},{24,16},{32,24},{40,32},{48,40},{56,48},{64,56},{72,6... | collective-permute-start | bytes 1572872 | tf_op jit(solution)/shard_map/while/body/eval_jaxpr/ppermute | solution.py:13
  365.9 28.8 %collective-permute-start = (bf16[256,1024]{1,0:T(8,128)(2,1)}, bf16[256,1024]{1,0:T(8,128)(2,1)}, u32[]{:S(2)}, u32[]{:S(2)}) collective-permute-start(bf16[256,1024]{1,0:T(8,128)(2,1)} %copy.23), channel_id=1, source_target_pairs={{8,0},{16,8},{24,16},{32,24},{40,32},{48,40},{56,48},{64,56},{72,6... | collective-permute-start | bytes 1572872 | tf_op jit(solution)/shard_map/while/body/eval_jaxpr/ppermute | solution.py:13
  396.6 28.8 %collective-permute-start = (bf16[256,1024]{1,0:T(8,128)(2,1)}, bf16[256,1024]{1,0:T(8,128)(2,1)}, u32[]{:S(2)}, u32[]{:S(2)}) collective-permute-start(bf16[256,1024]{1,0:T(8,128)(2,1)} %copy.23), channel_id=1, source_target_pairs={{8,0},{16,8},{24,16},{32,24},{40,32},{48,40},{56,48},{64,56},{72,6... | collective-permute-start | bytes 1572872 | tf_op jit(solution)/shard_map/while/body/eval_jaxpr/ppermute | solution.py:13
  427.3 28.8 %collective-permute-start = (bf16[256,1024]{1,0:T(8,128)(2,1)}, bf16[256,1024]{1,0:T(8,128)(2,1)}, u32[]{:S(2)}, u32[]{:S(2)}) collective-permute-start(bf16[256,1024]{1,0:T(8,128)(2,1)} %copy.23), channel_id=1, source_target_pairs={{8,0},{16,8},{24,16},{32,24},{40,32},{48,40},{56,48},{64,56},{72,6... | collective-permute-start | bytes 1572872 | tf_op jit(solution)/shard_map/while/body/eval_jaxpr/ppermute | solution.py:13
  457.9 28.8 %collective-permute-start = (bf16[256,1024]{1,0:T(8,128)(2,1)}, bf16[256,1024]{1,0:T(8,128)(2,1)}, u32[]{:S(2)}, u32[]{:S(2)}) collective-permute-start(bf16[256,1024]{1,0:T(8,128)(2,1)} %copy.23), channel_id=1, source_target_pairs={{8,0},{16,8},{24,16},{32,24},{40,32},{48,40},{56,48},{64,56},{72,6... | collective-permute-start | bytes 1572872 | tf_op jit(solution)/shard_map/while/body/eval_jaxpr/ppermute | solution.py:13
  488.6 28.8 %collective-permute-start = (bf16[256,1024]{1,0:T(8,128)(2,1)}, bf16[256,1024]{1,0:T(8,128)(2,1)}, u32[]{:S(2)}, u32[]{:S(2)}) collective-permute-start(bf16[256,1024]{1,0:T(8,128)(2,1)} %copy.23), channel_id=1, source_target_pairs={{8,0},{16,8},{24,16},{32,24},{40,32},{48,40},{56,48},{64,56},{72,6... | collective-permute-start | bytes 1572872 | tf_op jit(solution)/shard_map/while/body/eval_jaxpr/ppermute | solution.py:13
  519.2 28.8 %collective-permute-start = (bf16[256,1024]{1,0:T(8,128)(2,1)}, bf16[256,1024]{1,0:T(8,128)(2,1)}, u32[]{:S(2)}, u32[]{:S(2)}) collective-permute-start(bf16[256,1024]{1,0:T(8,128)(2,1)} %copy.23), channel_id=1, source_target_pairs={{8,0},{16,8},{24,16},{32,24},{40,32},{48,40},{56,48},{64,56},{72,6... | collective-permute-start | bytes 1572872 | tf_op jit(solution)/shard_map/while/body/eval_jaxpr/ppermute | solution.py:13
  549.9 28.8 %collective-permute-start = (bf16[256,1024]{1,0:T(8,128)(2,1)}, bf16[256,1024]{1,0:T(8,128)(2,1)}, u32[]{:S(2)}, u32[]{:S(2)}) collective-permute-start(bf16[256,1024]{1,0:T(8,128)(2,1)} %copy.23), channel_id=1, source_target_pairs={{8,0},{16,8},{24,16},{32,24},{40,32},{48,40},{56,48},{64,56},{72,6... | collective-permute-start | bytes 1572872 | tf_op jit(solution)/shard_map/while/body/eval_jaxpr/ppermute | solution.py:13
  580.5 28.8 %collective-permute-start = (bf16[256,1024]{1,0:T(8,128)(2,1)}, bf16[256,1024]{1,0:T(8,128)(2,1)}, u32[]{:S(2)}, u32[]{:S(2)}) collective-permute-start(bf16[256,1024]{1,0:T(8,128)(2,1)} %copy.23), channel_id=1, source_target_pairs={{8,0},{16,8},{24,16},{32,24},{40,32},{48,40},{56,48},{64,56},{72,6... | collective-permute-start | bytes 1572872 | tf_op jit(solution)/shard_map/while/body/eval_jaxpr/ppermute | solution.py:13
  611.2 28.8 %collective-permute-start = (bf16[256,1024]{1,0:T(8,128)(2,1)}, bf16[256,1024]{1,0:T(8,128)(2,1)}, u32[]{:S(2)}, u32[]{:S(2)}) collective-permute-start(bf16[256,1024]{1,0:T(8,128)(2,1)} %copy.23), channel_id=1, source_target_pairs={{8,0},{16,8},{24,16},{32,24},{40,32},{48,40},{56,48},{64,56},{72,6... | collective-permute-start | bytes 1572872 | tf_op jit(solution)/shard_map/while/body/eval_jaxpr/ppermute | solution.py:13
  649.0 1.6 copy-start
  649.0 2.2 copy-start.1
  652.6 93.0 %copy-start.3 = (f32[258,1024]{1,0:T(8,128)S(1)}, f32[258,1024]{1,0:T(8,128)}, u32[]{:S(2)}) copy-start(f32[258,1024]{1,0:T(8,128)} %copy-done.2) | copy-start | bytes 3170308
  748.6 1.0 copy-start.4
  749.6 56.3 %collective-permute-start.2 = (f32[2,1024]{1,0:T(2,128)S(1)}, f32[2,1024]{1,0:T(2,128)S(1)}, u32[]{:S(2)}, u32[]{:S(2)}) collective-permute-start(f32[2,1024]{1,0:T(2,128)S(1)} %slice.191), channel_id=1, source_target_pairs={{8,0},{16,8},{24,16},{32,24},{40,32},{48,40},{56,48},{64,56},{72,6... | collective-permute-start | bytes 24584 | tf_op jit(solution)/shard_map/ppermute | solution.py:13
Sparse Core Ops, SparseCore 0:
  14.4 149.0 all-gather.1
